TPU v7x, 32 devices: a whole 2x2x4 slice. The times are simulated.
32 devices in a mesh: cols: 2 (over x), sites: 16 (over z, y, core).
Axes of the slice: x: 2, y: 2, z: 4, core: 2. Of those that a mesh axis runs over, the one named last changes fastest.
Arguments:
- right_vectors: float32 [2, 64, 2, 16, 32, 256], P(None, None, None, None, ('cols', 'sites')), may hold values from -6 to 6
- left_vectors: bfloat16 [2, 64, 256, 512], P(None, None, 'sites'), may hold values from -0.015625 to 0.015625
- vacancy: int32 [256, 512], P('sites'), may hold values 0 or 1
Outputs:
- gamma_moments: float32 [2, 4, 64, 64, 2], P(None, None, None, None, 'cols')
All inputs are finite; a program needn't handle non-finite values. No bound on the sum of `vacancy` on one device may be relied on, other than what follows from the above.
Results may differ from a plain program's by a relative error of at most 0.0029.
Values sent between devices are 32-bit elements; how exact they have to be, the bound alone decides.
A program may use at most 128 MiB of HBM per device.

v0:
```python
import jax
import jax.numpy as jnp
from jax import lax
from jax.sharding import PartitionSpec as P

MOM = 4


ONSITE_MASS = 0.3
SECOND_HOP = 0.2
BAND_SCALE = 4.5


def padded_2(cells, sides, width):
    for axis, dim in sides:
        count = lax.axis_size(axis)
        head = lax.slice_in_dim(cells, 0, width, axis=dim)
        tail = lax.slice_in_dim(cells, cells.shape[dim] - width, cells.shape[dim], axis=dim)
        cells = jnp.concatenate(
            [
                lax.ppermute(tail, axis, [(i, (i + 1) % count) for i in range(count)]),
                cells,
                lax.ppermute(head, axis, [((i + 1) % count, i) for i in range(count)]),
            ],
            axis=dim,
        )
    return cells


def column_shift(values, offset):
    row_width = values.shape[-1]
    filler = jnp.zeros(values.shape[:-1] + (abs(offset),), values.dtype)
    if offset > 0:
        return jnp.concatenate([values[..., offset:], filler], axis=-1)
    return jnp.concatenate([filler, values[..., : row_width + offset]], axis=-1)


def rotate_phase(values):
    return jnp.stack([-values[1], values[0]])


def sign_table(row_count, row_width):
    rows_index = lax.broadcasted_iota(jnp.int32, (row_count, row_width), 0)
    cols_index = lax.broadcasted_iota(jnp.int32, (row_count, row_width), 1)
    return (1 - 2 * ((rows_index + cols_index) % 2)).astype(jnp.float32)


def haldane(padded, parity_sign):
    centre = padded[:, :, 1:-1, :]
    upper_row = padded[:, :, 2:, :]
    lower_row = padded[:, :, :-2, :]
    vertical = jnp.where(parity_sign > 0, upper_row, lower_row)
    nearest = column_shift(centre, 1) + column_shift(centre, -1) + vertical
    second = (
        column_shift(centre, 2)
        - column_shift(centre, -2)
        + column_shift(upper_row, -1)
        - column_shift(lower_row, 1)
        + column_shift(lower_row, -1)
        - column_shift(upper_row, 1)
    )
    return (
        ONSITE_MASS * parity_sign * centre
        + nearest
        + SECOND_HOP * parity_sign * rotate_phase(second)
    )


def velocity(padded, parity_sign):
    centre = padded[:, :, 1:-1, :]
    upper_row = padded[:, :, 2:, :]
    lower_row = padded[:, :, :-2, :]
    along_x = column_shift(centre, 1) - column_shift(centre, -1)
    farther = column_shift(centre, 2) + column_shift(centre, -2)
    diagonal = (
        column_shift(upper_row, 1)
        + column_shift(upper_row, -1)
        + column_shift(lower_row, 1)
        + column_shift(lower_row, -1)
    )
    return rotate_phase(along_x) - SECOND_HOP * parity_sign * (2.0 * farther - diagonal)


def with_rims(values):
    return padded_2(values, (("sites", 2),), 1)


def per_device(right_vectors, left_vectors, vacancy):
    layout = right_vectors.shape
    pieces = right_vectors.reshape(layout[0], layout[1], layout[2], layout[3], layout[5])
    slab_field = lax.all_to_all(
        lax.all_to_all(pieces, "cols", split_axis=2, concat_axis=2, tiled=True),
        "sites",
        split_axis=3,
        concat_axis=3,
        tiled=True,
    )
    row_count = left_vectors.shape[2]
    row_width = left_vectors.shape[3]
    count_left = left_vectors.shape[1]
    group_width = layout[1]
    site_count = row_count * row_width
    present = vacancy.astype(jnp.float32)
    current = slab_field.reshape(2, group_width, row_count, row_width) * present
    parity_sign = sign_table(row_count, row_width)
    latest = velocity(with_rims(current), parity_sign) * present
    previous = latest
    moment_list = [latest]
    for degree in range(1, MOM):
        applied = haldane(with_rims(latest), parity_sign) * present / BAND_SCALE
        following = applied if degree == 1 else 2.0 * applied - previous
        previous, latest = (latest, following)
        moment_list.append(latest)
    left_matrix = left_vectors.reshape(2 * count_left, site_count)
    summed_list = []
    for moment in moment_list:
        rounded = moment.astype(jnp.bfloat16).reshape(2 * group_width, site_count)
        product = lax.dot_general(
            left_matrix, rounded, (((1,), (1,)), ((), ())), preferred_element_type=jnp.float32
        ).reshape(2, count_left, 2, group_width)
        combined = jnp.stack(
            [product[0, :, 0] + product[1, :, 1], product[0, :, 1] - product[1, :, 0]]
        )
        summed_list.append(lax.psum(combined, "sites"))
    summed = jnp.stack(summed_list, axis=1)
    return summed[..., None]


def solution(mesh):
    return jax.shard_map(
        per_device,
        mesh=mesh,
        in_specs=(
            P(None, None, None, None, ("cols", "sites"), None),
            P(None, None, "sites", None),
            P("sites", None),
        ),
        out_specs=P(None, None, None, None, "cols"),
        check_vma=False,
    )
```

profile of v0, /device:TPU:0, one launch (start us, length us, event | category | flops | bytes accessed | tf_op | source)
XLA Modules:
  0.0 468.4 jit_solution(6814094422640097991)
XLA Ops:
  9.3 51.5 %all_to_all.10 = f32[2,64,2,16,256]{4,3,1,0,2:T(8,128)S(1)} all-to-all(f32[2,64,2,16,256]{4,3,1,0,2:T(8,128)S(1)} %bitcast.73), channel_id=1, replica_groups=mesh['cols'=2,'sites'=16] {'cols'}, dimensions={2} | all-to-all | bytes 8388608 | tf_op jit(solution)/shard_map/all_to_all | solution.py:92
  60.8 5.2 %copy.39 = f32[2,64,2,16,256]{4,2,1,0,3:T(2,128)} copy(f32[2,64,2,16,256]{4,3,1,0,2:T(8,128)S(1)} %all_to_all.10) | data formatting | bytes 8388608 | tf_op jit(solution)/shard_map/all_to_all | solution.py:92
  66.1 6.4 %all-to-all-start.1 = ((f32[2,64,2,16,256]{4,2,1,0,3:T(2,128)}), f32[2,64,2,16,256]{4,2,1,0,3:T(2,128)}, u32[]{:S(2)}, u32[]{:S(2)}) async-start(f32[2,64,2,16,256]{4,2,1,0,3:T(2,128)} %copy.39), calls=%async_computation.1 | async-start | bytes 8388608 | tf_op jit(solution)/shard_map/all_to_all | solution.py:91
  75.6 74.5 %all-to-all-done.1 = f32[2,64,2,16,256]{4,2,1,0,3:T(2,128)} async-done(((f32[2,64,2,16,256]{4,2,1,0,3:T(2,128)}), f32[2,64,2,16,256]{4,2,1,0,3:T(2,128)}, u32[]{:S(2)}, u32[]{:S(2)}) %all-to-all-start.1) | async-done | bytes 4194336 | tf_op jit(solution)/shard_map/all_to_all | solution.py:91
  150.1 6.6 %copy.40 = f32[2,64,2,16,256]{4,3,2,1,0:T(8,128)} copy(f32[2,64,2,16,256]{4,2,1,0,3:T(2,128)} %all-to-all-done.1) | data formatting | bytes 8388608 | tf_op jit(solution)/shard_map/all_to_all | solution.py:91
  156.7 5.2 %reshape.206 = f32[2,64,16,512]{3,2,1,0:T(8,128)} reshape(f32[2,64,2,16,256]{4,3,2,1,0:T(8,128)} %copy.40) | data formatting | bytes 8388608 | tf_op jit(solution)/shard_map/reshape | solution.py:104
  165.2 18.2 %collective-permute-start = (f32[2,64,1,512]{3,2,1,0:T(1,128)S(1)}, f32[2,64,1,512]{3,2,1,0:T(1,128)S(1)}, u32[]{:S(2)}, u32[]{:S(2)}) collective-permute-start(f32[2,64,1,512]{3,2,1,0:T(1,128)S(1)} %get-tuple-element.53), channel_id=1, source_target_pairs={{1,0},{2,1},{3,2},{4,3},{5,4},{6,5},{7,6},{8,7},{9,8},{10,9},{11,1... | collective-permute-start | bytes 786440 | tf_op jit(solution)/shard_map/ppermute | solution.py:23
  183.4 4.8 %fusion.72 = (f32[2,64,16,510]{3,2,1,0:T(8,128)}, f32[2,64,16,510]{3,2,1,0:T(8,128)}) fusion(f32[2,64,16,512]{3,2,1,0:T(8,128)S(1)} %broadcast_multiply_fusion.1), kind=kLoop, calls=%fused_computation.143 | loop fusion | bytes 16711680 | tf_op jit(solution)/shard_map/slice | solution.py:34
  188.2 3.7 collective-permute-done.1
  191.9 7.9 %fusion.71 = (f32[2,64,16,511]{3,2,1,0:T(8,128)S(1)}, f32[2,64,16,511]{3,2,1,0:T(8,128)}, f32[2,64,16,511]{3,2,1,0:T(8,128)}, f32[2,64,16,511]{3,2,1,0:T(8,128)S(1)}) fusion(f32[2,64,16,512]{3,2,1,0:T(8,128)S(1)} %broadcast_multiply_fusion.1, f32[2,64,1,512]{3,2,1,0:T(1,128)S(1)} %collective-permute-done.1, f32[2,64,1,512]{3,2,1,0:T(1,128)S(1)} %collective-permute-done), kind=kLoop, calls=%fused_computation.142 | loop fusion | flops 2093056 | bytes 29851648 | tf_op jit(solution)/shard_map/slice | solution.py:34
  199.8 3.1 fusion.48
  202.9 9.8 %fusion.57 = (bf16[2,64,16,512]{3,2,1,0:T(8,128)(2,1)S(1)}, f32[2,64,16,512]{3,2,1,0:T(8,128)S(1)}) fusion(f32[16,512]{1,0:T(8,128)S(1)} %convert_element_type.43, f32[2,64,16,512]{3,2,1,0:T(8,128)S(1)} %broadcast_multiply_fusion.1, f32[2,64,1,512]{3,2,1,0:T(1,128)S(1)} %collective-permute-done.1, f32[2,64,16,511]{3,2,1,0:T(8,128)} %get-tuple-element.48, ...), kind=kLoop, calls=%fused_computation.131 | loop fusion | flops 18874368 | bytes 31997952 | tf_op jit(solution)/shard_map/convert_element_type | solution.py:117
  213.2 4.7 %fusion.69 = (f32[2,64,16,510]{3,2,1,0:T(8,128)}, f32[2,64,16,510]{3,2,1,0:T(8,128)}) fusion(f32[2,64,16,512]{3,2,1,0:T(8,128)S(1)} %get-tuple-element.10), kind=kLoop, calls=%fused_computation.140 | loop fusion | bytes 16711680 | tf_op jit(solution)/shard_map/slice | solution.py:34
  222.1 3.2 collective-permute-done.2
  225.3 4.6 collective-permute-done.3
  229.9 13.2 %fusion.68 = (f32[2,64,16,511]{3,2,1,0:T(8,128)}, f32[2,64,16,511]{3,2,1,0:T(8,128)S(1)}, f32[2,64,16,511]{3,2,1,0:T(8,128)S(1)}, f32[2,64,16,511]{3,2,1,0:T(8,128)}) fusion(f32[2,64,16,512]{3,2,1,0:T(8,128)} %copy-done, f32[2,64,1,512]{3,2,1,0:T(1,128)S(1)} %collective-permute-done.3, f32[2,64,1,512]{3,2,1,0:T(1,128)S(1)} %collective-permute-done.2), kind=kLoop, calls=%fused_computation.139 | loop fusion | flops 2093056 | bytes 29851648 | tf_op jit(solution)/shard_map/slice | solution.py:34
  243.1 8.6 %fusion.38 = f32[2,64,16,512]{3,2,1,0:T(8,128)S(1)} fusion(f32[2,64,1,512]{3,2,1,0:T(1,128)S(1)} %collective-permute-done.2, f32[2,64,16,512]{3,2,1,0:T(8,128)S(1)} %copy-done.1, f32[2,64,1,512]{3,2,1,0:T(1,128)S(1)} %collective-permute-done.3, f32[2,64,16,511]{3,2,1,0:T(8,128)S(1)} %get-tuple-element.38, f32[2,64,16,511]{3,2,1,0:T(8,128)S(1)} %get-tuple-element.39, ...), kind=kLoop, calls=%fused_computation.71 | loop fusion | flops 13631488 | bytes 25640960 | tf_op jit(solution)/shard_map/sub | solution.py:55
  255.4 6.1 %fusion.56 = (bf16[2,64,16,512]{3,2,1,0:T(8,128)(2,1)S(1)}, f32[2,64,16,512]{3,2,1,0:T(8,128)S(1)}) fusion(f32[16,512]{1,0:T(8,128)S(1)} %convert_element_type.43, f32[1,64,16,512]{3,2,1,0:T(8,128)} %get-tuple-element.42, f32[1,64,16,512]{3,2,1,0:T(8,128)} %get-tuple-element.41, f32[16,512]{1,0:T(8,128)S(1)} %broadcast_multiply_fusion.4, ...), kind=kLoop, calls=%fused_computation.130 | loop fusion | flops 13631488 | bytes 23683072 | tf_op jit(solution)/shard_map/convert_element_type | solution.py:117
  265.2 4.8 %fusion.66 = (f32[2,64,16,510]{3,2,1,0:T(8,128)}, f32[2,64,16,510]{3,2,1,0:T(8,128)}) fusion(f32[2,64,16,512]{3,2,1,0:T(8,128)S(1)} %broadcast_multiply_fusion), kind=kLoop, calls=%fused_computation.137 | loop fusion | bytes 16711680 | tf_op jit(solution)/shard_map/slice | solution.py:34
  273.9 3.1 collective-permute-done.4
  276.9 4.3 collective-permute-done.5
  281.3 13.4 %fusion.65 = (f32[2,64,16,511]{3,2,1,0:T(8,128)}, f32[2,64,16,511]{3,2,1,0:T(8,128)S(1)}, f32[2,64,16,511]{3,2,1,0:T(8,128)S(1)}, f32[2,64,16,511]{3,2,1,0:T(8,128)}) fusion(f32[2,64,16,512]{3,2,1,0:T(8,128)} %copy-done.3, f32[2,64,1,512]{3,2,1,0:T(1,128)S(1)} %collective-permute-done.5, f32[2,64,1,512]{3,2,1,0:T(1,128)S(1)} %collective-permute-done.4), kind=kLoop, calls=%fused_computation.136 | loop fusion | flops 2093056 | bytes 29851648 | tf_op jit(solution)/shard_map/slice | solution.py:34
  294.6 9.4 %fusion.36 = f32[2,64,16,512]{3,2,1,0:T(8,128)} fusion(f32[2,64,1,512]{3,2,1,0:T(1,128)S(1)} %collective-permute-done.4, f32[2,64,16,512]{3,2,1,0:T(8,128)S(1)} %copy-done.4, f32[2,64,1,512]{3,2,1,0:T(1,128)S(1)} %collective-permute-done.5, f32[2,64,16,511]{3,2,1,0:T(8,128)S(1)} %get-tuple-element.28, f32[2,64,16,511]{3,2,1,0:T(8,128)S(1)} %get-tuple-element.29, ...), kind=kLoop, calls=%fused_computation.67 | loop fusion | flops 13631488 | bytes 25640960 | tf_op jit(solution)/shard_map/sub | solution.py:55
  304.0 5.3 %slice_negate_fusion.1 = (f32[1,64,16,512]{3,2,1,0:T(8,128)}, f32[1,64,16,512]{3,2,1,0:T(8,128)}) fusion(f32[2,64,16,512]{3,2,1,0:T(8,128)} %fusion.36), kind=kLoop, calls=%fused_computation.94 | loop fusion | flops 524288 | bytes 8388608 | tf_op jit(solution)/shard_map/neg | solution.py:39
  309.8 8.6 %fusion.60 = (bf16[2,64,16,512]{3,2,1,0:T(8,128)(2,1)}, f32[2,64,16,512]{3,2,1,0:T(8,128)S(1)}) fusion(f32[2,64,16,512]{3,2,1,0:T(8,128)S(1)} %copy-done.2, f32[16,512]{1,0:T(8,128)S(1)} %convert_element_type.43, f32[1,64,16,512]{3,2,1,0:T(8,128)} %get-tuple-element.32, f32[1,64,16,512]{3,2,1,0:T(8,128)} %get-tuple-element.31, ...), kind=kLoop, calls=%fused_computation.132 | loop fusion | flops 14680064 | bytes 32071680 | tf_op jit(solution)/shard_map/convert_element_type | solution.py:117
  319.0 4.8 %fusion.63 = (f32[2,64,16,510]{3,2,1,0:T(8,128)}, f32[2,64,16,510]{3,2,1,0:T(8,128)}) fusion(f32[2,64,16,512]{3,2,1,0:T(8,128)S(1)} %get-tuple-element.14), kind=kLoop, calls=%fused_computation.134 | loop fusion | bytes 16711680 | tf_op jit(solution)/shard_map/slice | solution.py:34
  330.7 4.6 collective-permute-done.7
  335.3 12.8 %fusion.62 = (f32[2,64,16,511]{3,2,1,0:T(8,128)}, f32[2,64,16,511]{3,2,1,0:T(8,128)S(1)}, f32[2,64,16,511]{3,2,1,0:T(8,128)S(1)}, f32[2,64,16,511]{3,2,1,0:T(8,128)}) fusion(f32[2,64,16,512]{3,2,1,0:T(8,128)} %copy-done.5, f32[2,64,1,512]{3,2,1,0:T(1,128)S(1)} %collective-permute-done.7, f32[2,64,1,512]{3,2,1,0:T(1,128)S(1)} %collective-permute-done.6), kind=kLoop, calls=%fused_computation.133 | loop fusion | flops 2093056 | bytes 29851648 | tf_op jit(solution)/shard_map/slice | solution.py:34
  348.2 10.0 %fusion.34 = f32[2,64,16,512]{3,2,1,0:T(8,128)} fusion(f32[2,64,1,512]{3,2,1,0:T(1,128)S(1)} %collective-permute-done.6, f32[2,64,16,512]{3,2,1,0:T(8,128)S(1)} %copy-done.6, f32[2,64,1,512]{3,2,1,0:T(1,128)S(1)} %collective-permute-done.7, f32[2,64,16,511]{3,2,1,0:T(8,128)S(1)} %get-tuple-element.18, f32[2,64,16,511]{3,2,1,0:T(8,128)S(1)} %get-tuple-element.19, ...), kind=kLoop, calls=%fused_computation.63 | loop fusion | flops 13631488 | bytes 25640960 | tf_op jit(solution)/shard_map/sub | solution.py:55
  358.1 5.2 %slice_negate_fusion = (f32[1,64,16,512]{3,2,1,0:T(8,128)}, f32[1,64,16,512]{3,2,1,0:T(8,128)}) fusion(f32[2,64,16,512]{3,2,1,0:T(8,128)} %fusion.34), kind=kLoop, calls=%fused_computation.93 | loop fusion | flops 524288 | bytes 8388608 | tf_op jit(solution)/shard_map/neg | solution.py:39
  363.9 6.7 %fusion.11 = bf16[2,64,16,512]{3,2,1,0:T(8,128)(2,1)S(1)} fusion(f32[2,64,16,512]{3,2,1,0:T(8,128)S(1)} %copy-done.6, f32[2,64,1,512]{3,2,1,0:T(1,128)S(1)} %collective-permute-done.7, f32[2,64,1,512]{3,2,1,0:T(1,128)S(1)} %collective-permute-done.6, f32[1,64,16,512]{3,2,1,0:T(8,128)} %get-tuple-element.22, f32[1,64,16,512]{3,2,1,0:T(8,128)} %get-tuple-element.21, ...), kind=kLoop, calls=%fused_computation.39 | loop fusion | flops 15728640 | bytes 23683072 | tf_op jit(solution)/shard_map/convert_element_type | solution.py:117
  374.0 85.7 %all-reduce.35.cloned.1.call-done = (f32[2,1,64,64]{3,2,1,0:T(8,128)}, f32[2,1,64,64]{3,2,1,0:T(8,128)}, f32[2,1,64,64]{3,2,1,0:T(8,128)}, f32[2,1,64,64]{3,2,1,0:T(8,128)}) async-done(((f32[2,1,64,64]{3,2,1,0:T(8,128)}, f32[2,1,64,64]{3,2,1,0:T(8,128)}, f32[2,1,64,64]{3,2,1,0:T(8,128)}, f32[2,1,64,64]{3,2,1,0:T(8,128)}), (f32[2,1,64,64]{3,2,1,0:T(8,128)}, f32[2,1,64,64]{3,2,1,0:T(8,128)}, ...) | async-done | bytes 131088 | tf_op jit(solution)/shard_map/psum | solution.py:124
  (100 shorter events, 38.3 us)
Async XLA Ops:
  66.1 6.4 %copy-start.16 = (s32[16,512]{1,0:T(8,128)S(1)}, s32[16,512]{1,0:T(8,128)}, u32[]{:S(2)}) copy-start(s32[16,512]{1,0:T(8,128)} %param.5) | copy-start | bytes 98308
  66.1 84.0 %all-to-all-start.1 = ((f32[2,64,2,16,256]{4,2,1,0,3:T(2,128)}), f32[2,64,2,16,256]{4,2,1,0,3:T(2,128)}, u32[]{:S(2)}, u32[]{:S(2)}) async-start(f32[2,64,2,16,256]{4,2,1,0,3:T(2,128)} %copy.39), calls=%async_computation.1 | async-start | bytes 8388608 | tf_op jit(solution)/shard_map/all_to_all | solution.py:91
  72.4 387.2 %all-reduce.35.cloned.1.call-start = ((), (), s32[]{:S(2)}) async-start(), calls=%async_computation.2 | async-start | bytes 524288 | tf_op jit(solution)/shard_map/psum | solution.py:124
  75.5 195.9 %copy-start.10 = (bf16[16,8,16,512]{3,1,2,0:T(8,128)(2,1)}, bf16[16,8,16,512]{3,1,2,0:T(8,128)(2,1)S(1)}, u32[]{:S(2)}) copy-start(bf16[16,8,16,512]{3,1,2,0:T(8,128)(2,1)S(1)} %copy.74) | copy-start | bytes 6291460
  165.2 23.0 %collective-permute-start = (f32[2,64,1,512]{3,2,1,0:T(1,128)S(1)}, f32[2,64,1,512]{3,2,1,0:T(1,128)S(1)}, u32[]{:S(2)}, u32[]{:S(2)}) collective-permute-start(f32[2,64,1,512]{3,2,1,0:T(1,128)S(1)} %get-tuple-element.53), channel_id=1, source_target_pairs={{1,0},{2,1},{3,2},{4,3},{5,4},{6,5},{7,6},{8,7},{9,8},{10,9},{11,1... | collective-permute-start | bytes 786440 | tf_op jit(solution)/shard_map/ppermute | solution.py:23
  183.4 8.5 %collective-permute-start.1 = (f32[2,64,1,512]{3,2,1,0:T(1,128)S(1)}, f32[2,64,1,512]{3,2,1,0:T(1,128)S(1)}, u32[]{:S(2)}, u32[]{:S(2)}) collective-permute-start(f32[2,64,1,512]{3,2,1,0:T(1,128)S(1)} %get-tuple-element.54), channel_id=1, source_target_pairs={{0,1},{1,2},{2,3},{3,4},{4,5},{5,6},{6,7},{7,8},{8,9},{9,10},{10,1... | collective-permute-start | bytes 786440 | tf_op jit(solution)/shard_map/ppermute | solution.py:21
  212.7 5.3 %copy-start = (f32[2,64,16,512]{3,2,1,0:T(8,128)}, f32[2,64,16,512]{3,2,1,0:T(8,128)S(1)}, u32[]{:S(2)}) copy-start(f32[2,64,16,512]{3,2,1,0:T(8,128)S(1)} %get-tuple-element.10) | copy-start | bytes 12582916
  220.6 4.7 collective-permute-start.2
  221.4 8.5 %collective-permute-start.3 = (f32[2,64,1,512]{3,2,1,0:T(1,128)S(1)}, f32[2,64,1,512]{3,2,1,0:T(1,128)S(1)}, u32[]{:S(2)}, u32[]{:S(2)}) collective-permute-start(f32[2,64,1,512]{3,2,1,0:T(1,128)S(1)} %get-tuple-element.45), channel_id=1, source_target_pairs={{0,1},{1,2},{2,3},{3,4},{4,5},{5,6},{6,7},{7,8},{8,9},{9,10},{10,1... | collective-permute-start | bytes 786440 | tf_op jit(solution)/shard_map/ppermute | solution.py:21
  222.1 21.0 %copy-start.1 = (f32[2,64,16,512]{3,2,1,0:T(8,128)S(1)}, f32[2,64,16,512]{3,2,1,0:T(8,128)}, u32[]{:S(2)}) copy-start(f32[2,64,16,512]{3,2,1,0:T(8,128)} %copy-done) | copy-start | bytes 12582916
  251.7 3.7 copy-start.14
  261.6 2.0 copy-start.7
  263.6 6.4 %copy-start.3 = (f32[2,64,16,512]{3,2,1,0:T(8,128)}, f32[2,64,16,512]{3,2,1,0:T(8,128)S(1)}, u32[]{:S(2)}) copy-start(f32[2,64,16,512]{3,2,1,0:T(8,128)S(1)} %broadcast_multiply_fusion) | copy-start | bytes 12582916
  272.7 4.3 collective-permute-start.4
  272.7 8.5 %collective-permute-start.5 = (f32[2,64,1,512]{3,2,1,0:T(1,128)S(1)}, f32[2,64,1,512]{3,2,1,0:T(1,128)S(1)}, u32[]{:S(2)}, u32[]{:S(2)}) collective-permute-start(f32[2,64,1,512]{3,2,1,0:T(1,128)S(1)} %get-tuple-element.35), channel_id=1, source_target_pairs={{0,1},{1,2},{2,3},{3,4},{4,5},{5,6},{6,7},{7,8},{8,9},{9,10},{10,1... | collective-permute-start | bytes 786440 | tf_op jit(solution)/shard_map/ppermute | solution.py:21
  273.9 20.8 %copy-start.4 = (f32[2,64,16,512]{3,2,1,0:T(8,128)S(1)}, f32[2,64,16,512]{3,2,1,0:T(8,128)}, u32[]{:S(2)}) copy-start(f32[2,64,16,512]{3,2,1,0:T(8,128)} %copy-done.3) | copy-start | bytes 12582916
  273.9 20.8 %copy-start.12 = (f32[2,64,16,510]{3,2,1,0:T(8,128)S(1)}, f32[2,64,16,510]{3,2,1,0:T(8,128)}, u32[]{:S(2)}) copy-start(f32[2,64,16,510]{3,2,1,0:T(8,128)} %get-tuple-element.33) | copy-start | bytes 12533764
  304.0 5.3 %copy-start.2 = (f32[2,64,16,512]{3,2,1,0:T(8,128)S(1)}, f32[2,64,16,512]{3,2,1,0:T(8,128)}, u32[]{:S(2)}) copy-start(f32[2,64,16,512]{3,2,1,0:T(8,128)} %copy-done) | copy-start | bytes 12582916
  304.0 5.8 %copy-start.8 = (f32[2,64,16,512]{3,2,1,0:T(8,128)S(1)}, f32[2,64,16,512]{3,2,1,0:T(8,128)}, u32[]{:S(2)}) copy-start(f32[2,64,16,512]{3,2,1,0:T(8,128)} %copy-done.7) | copy-start | bytes 12582916
  318.4 5.3 %copy-start.5 = (f32[2,64,16,512]{3,2,1,0:T(8,128)}, f32[2,64,16,512]{3,2,1,0:T(8,128)S(1)}, u32[]{:S(2)}) copy-start(f32[2,64,16,512]{3,2,1,0:T(8,128)S(1)} %get-tuple-element.14) | copy-start | bytes 12582916
  318.9 4.8 %copy-start.15 = (bf16[2,64,16,512]{3,2,1,0:T(8,128)(2,1)S(1)}, bf16[2,64,16,512]{3,2,1,0:T(8,128)(2,1)}, u32[]{:S(2)}) copy-start(bf16[2,64,16,512]{3,2,1,0:T(8,128)(2,1)} %get-tuple-element.13) | copy-start | bytes 6291460
  323.7 1.6 copy-start.11
  326.6 4.1 collective-permute-start.6
  326.8 8.5 %collective-permute-start.7 = (f32[2,64,1,512]{3,2,1,0:T(1,128)S(1)}, f32[2,64,1,512]{3,2,1,0:T(1,128)S(1)}, u32[]{:S(2)}, u32[]{:S(2)}) collective-permute-start(f32[2,64,1,512]{3,2,1,0:T(1,128)S(1)} %get-tuple-element.26), channel_id=1, source_target_pairs={{0,1},{1,2},{2,3},{3,4},{4,5},{5,6},{6,7},{7,8},{8,9},{9,10},{10,1... | collective-permute-start | bytes 786440 | tf_op jit(solution)/shard_map/ppermute | solution.py:21
  327.8 20.4 %copy-start.6 = (f32[2,64,16,512]{3,2,1,0:T(8,128)S(1)}, f32[2,64,16,512]{3,2,1,0:T(8,128)}, u32[]{:S(2)}) copy-start(f32[2,64,16,512]{3,2,1,0:T(8,128)} %copy-done.5) | copy-start | bytes 12582916
  358.1 5.2 %copy-start.9 = (f32[2,64,16,512]{3,2,1,0:T(8,128)S(1)}, f32[2,64,16,512]{3,2,1,0:T(8,128)}, u32[]{:S(2)}) copy-start(f32[2,64,16,512]{3,2,1,0:T(8,128)} %copy-done.7) | copy-start | bytes 12582916
  358.1 5.8 %copy-start.13 = (f32[2,64,16,511]{3,2,1,0:T(8,128)S(1)}, f32[2,64,16,511]{3,2,1,0:T(8,128)}, u32[]{:S(2)}) copy-start(f32[2,64,16,511]{3,2,1,0:T(8,128)} %get-tuple-element.17) | copy-start | bytes 12558340
Sparse Core Ops, SparseCore 0:
  374.1 85.5 all-reduce.34
where the time goes:
time: 477 us; the launch traced here: 468 us
  waiting for transfers between devices  187 us (39%)
  other arithmetic  130 us (27%)
  local copies, waits for them, and re-layouts  56.5 us (12%)
  blocking collectives  51.5 us (11%)
  starting transfers between devices  26.5 us (6%)
  between operations  13.9 us (3%)
    psum x1, waiting for transfers between devices, per_device(): summed_list.append(lax.psum(combined, 'sites'))  85.7 us
    all_to_all x1, waiting for transfers between devices, per_device(): lax.all_to_all(lax.all_to_all(pieces, 'cols', split_axis=2, concat_axis=2...  74.5 us
    all_to_all x1, blocking collectives, per_device(): lax.all_to_all(pieces, 'cols', split_axis=2, concat_axis=2, tiled=True)  51.5 us
    slice x4, other arithmetic, column_shift(): return jnp.concatenate([values[..., offset:], filler], axis=-1)  47.3 us
    convert_element_type x4, other arithmetic, per_device(): rounded = moment.astype(jnp.bfloat16).reshape(2 * group_width, site_count)  31.3 us
    sub x3, other arithmetic, haldane(): column_shift(centre, 2) - column_shift(centre, -2)  28 us
    ppermute x4, starting transfers between devices, padded_2(): lax.ppermute(head, axis, [((i + 1) % count, i) for i in range(count)])  19.3 us
    slice x4, local copies, waits for them, and re-layouts, column_shift(): return jnp.concatenate([values[..., offset:], filler], axis=-1)  19 us
  transfers between devices with their start and end apart: 10, of which 9 were waited for; matrix products, arithmetic and copies ran while one was open for 2% of the time, Pallas kernels for 0%

commit v1 on v0

--- a/solution.py
+++ b/solution.py
@@ -1,6 +1,10 @@
+import functools
+
 import jax
 import jax.numpy as jnp
 from jax import lax
+from jax.experimental import pallas as pl
+from jax.experimental.pallas import tpu as pltpu
 from jax.sharding import PartitionSpec as P
 
 MOM = 4
@@ -85,7 +89,7 @@
     return padded_2(values, (("sites", 2),), 1)
 
 
-def per_device(right_vectors, left_vectors, vacancy):
+def per_device_plain(right_vectors, left_vectors, vacancy):
     layout = right_vectors.shape
     pieces = right_vectors.reshape(layout[0], layout[1], layout[2], layout[3], layout[5])
     slab_field = lax.all_to_all(
@@ -126,9 +130,336 @@
     return summed[..., None]
 
 
+MESH = pl.DeviceIdType.MESH
+HALO = MOM
+COLS_AT_ONCE = 16
+
+
+def fused_kernel(
+    groups, sites, right_ref, left_ref, vacancy_ref, out_ref,
+    arrived, field0, field1, field2, field3, present, scaled, doubled, rounded,
+    partial, shares, total,
+    piece_send, piece_recv, rim_send, rim_recv, mask_send, mask_recv,
+    share_send, share_recv, total_send, total_recv,
+):
+    chunks, padded_rows, _, wide, width = arrived.shape
+    rows = padded_rows - 2 * HALO
+    piece = right_ref.shape[5]
+    per_row = width // piece
+    count = groups * sites
+    my_group, my_site = lax.axis_index("cols"), lax.axis_index("sites")
+    mine = my_group * sites + my_site
+    above, below = lax.rem(my_site + 1, sites), lax.rem(my_site + sites - 1, sites)
+
+    barrier = pltpu.get_barrier_semaphore()
+
+    def greet(step, carry):
+        other = lax.rem(mine + step, count)
+        pl.semaphore_signal(
+            barrier, inc=1, device_id={"cols": other // sites, "sites": lax.rem(other, sites)}, device_id_type=MESH
+        )
+        return carry
+
+    lax.fori_loop(1, count, greet, 0)
+
+    lane = lax.broadcasted_iota(jnp.int32, (8, width), 1)
+    odd_lane = lax.rem(lane, 2) == 1
+
+    for row in range(rows):
+        present[HALO + row] = jnp.broadcast_to(vacancy_ref[row : row + 1, :].astype(jnp.float32), (8, width))
+
+    pl.semaphore_wait(barrier, count - 1)
+
+    def landing(chunk, run):
+        return arrived.at[
+            chunk, HALO + run // per_row, :, :, pl.ds(pl.multiple_of(lax.rem(run, per_row) * piece, piece), piece)
+        ]
+
+    def piece_of(chunk, group, site):
+        return right_ref.at[:, pl.ds(pl.multiple_of(chunk * wide, wide), wide), group, site, 0, :]
+
+    def piece_copy(chunk, step):
+        other = lax.rem(mine + step, count)
+        group, site = other // sites, lax.rem(other, sites)
+        return pltpu.make_async_remote_copy(
+            src_ref=piece_of(chunk, group, site),
+            dst_ref=landing(chunk, mine),
+            send_sem=piece_send.at[chunk, step],
+            recv_sem=piece_recv.at[chunk],
+            device_id={"cols": group, "sites": site},
+            device_id_type=MESH,
+        )
+
+    def rim_copy(source, send_sem, recv_sem, up):
+        first = rows if up else HALO
+        landing_row = 0 if up else rows + HALO
+        return pltpu.make_async_remote_copy(
+            src_ref=source.at[pl.ds(first, HALO)],
+            dst_ref=source.at[pl.ds(landing_row, HALO)],
+            send_sem=send_sem,
+            recv_sem=recv_sem,
+            device_id={"sites": above if up else below},
+            device_id_type=MESH,
+        )
+
+    def mask_copies():
+        return [rim_copy(present, mask_send.at[i], mask_recv.at[i], up) for i, up in enumerate((True, False))]
+
+    def rim_copies(chunk):
+        return [
+            rim_copy(arrived.at[chunk], rim_send.at[chunk, i], rim_recv.at[chunk, i], up)
+            for i, up in enumerate((True, False))
+        ]
+
+    for copy in mask_copies():
+        copy.start()
+
+    def send_chunk(chunk, carry):
+        def send(step, inner):
+            piece_copy(chunk, step).start()
+            return inner
+
+        lax.fori_loop(1, count, send, 0)
+        pltpu.make_async_copy(piece_of(chunk, my_group, my_site), landing(chunk, mine), piece_recv.at[chunk]).start()
+        return carry
+
+    lax.fori_loop(0, chunks, send_chunk, 0)
+
+    for copy in mask_copies():
+        copy.wait()
+
+    def scale_masks(row, carry):
+        held = present[row]
+        scaled[row] = held * (1.0 / BAND_SCALE)
+        doubled[row] = held * (2.0 / BAND_SCALE)
+        return carry
+
+    lax.fori_loop(0, padded_rows, scale_masks, 0)
+
+    def shift(values, offset):
+        turned = pltpu.roll(values, width - 1 if offset > 0 else 1, axis=1)
+        return jnp.where(lane == (width - 1 if offset > 0 else 0), 0.0, turned)
+
+    def signed(values, odd_row):
+        return jnp.where(odd_lane != odd_row, -values, values)
+
+    def sweep(source, target, earlier, mask, degree):
+        first = degree + 1
+
+        def one_row(row, odd_row):
+            halves = [[], []]
+            for part in range(0, wide, 8):
+                at = slice(part, part + 8)
+                centre = [source[row, r, at, :] for r in (0, 1)]
+                upper = [source[row + 1, r, at, :] for r in (0, 1)]
+                lower = [source[row - 1, r, at, :] for r in (0, 1)]
+                right = [shift(c, 1) for c in centre]
+                left = [shift(c, -1) for c in centre]
+                both = [u + l for u, l in zip(upper, lower)]
+                if degree == 0:
+                    far = [shift(2.0 * a - s, 1) + shift(2.0 * b - s, -1) for a, b, s in zip(right, left, both)]
+                    near = [a - b for a, b in zip(right, left)]
+                    applied = [
+                        -near[1] - signed(SECOND_HOP * far[0], odd_row),
+                        near[0] - signed(SECOND_HOP * far[1], odd_row),
+                    ]
+                else:
+                    far = [shift(a - s, 1) - shift(b - s, -1) for a, b, s in zip(right, left, both)]
+                    phase = [-far[1], far[0]]
+                    applied = [
+                        signed(ONSITE_MASS * centre[r] + SECOND_HOP * phase[r], odd_row)
+                        + (right[r] + left[r])
+                        + jnp.where(odd_lane != odd_row, lower[r], upper[r])
+                        for r in (0, 1)
+                    ]
+                factor = mask[row]
+                for r in (0, 1):
+                    result = applied[r] * factor
+                    if earlier is not None:
+                        result = result - earlier[row, r, at, :]
+                    if target is not None:
+                        target[row, r, at, :] = result
+                    halves[r].append(result)
+            lanes = pl.ds(pl.multiple_of(row * width, width), width)
+            for r in (0, 1):
+                base = (r * MOM + degree) * wide
+                rounded[base : base + wide, lanes] = jnp.concatenate(halves[r], axis=0).astype(jnp.bfloat16)
+
+        def pair(step, carry):
+            one_row(first + 2 * step, first % 2 == 1)
+            one_row(first + 2 * step + 1, first % 2 == 0)
+            return carry
+
+        lax.fori_loop(0, (padded_rows - 2 * first) // 2, pair, 0)
+
+    def stage(chunk):
+        held = arrived.at[chunk, pl.ds(HALO, rows)]
+        pltpu.make_async_copy(held, held, piece_recv.at[chunk]).wait()
+        for copy in rim_copies(chunk):
+            copy.start()
+
+    def compute(chunk):
+        for copy in rim_copies(chunk):
+            copy.wait()
+
+        def mask_row(row, carry):
+            for r in (0, 1):
+                for part in range(0, wide, 8):
+                    at = slice(part, part + 8)
+                    field0[row, r, at, :] = arrived[chunk, row, r, at, :] * present[row]
+            return carry
+
+        lax.fori_loop(0, padded_rows, mask_row, 0)
+        sweep(field0, field1, None, present, 0)
+        sweep(field1, field2, None, scaled, 1)
+        sweep(field2, field3, field1, doubled, 2)
+        sweep(field3, None, field2, doubled, 3)
+        product = lax.dot_general(
+            left_ref[...],
+            rounded[:, HALO * width : (HALO + rows) * width],
+            (((1,), (1,)), ((), ())),
+            preferred_element_type=jnp.float32,
+        )
+        count_left = product.shape[0] // 2
+        half = product.shape[1] // 2
+        real, imaginary = product[:count_left], product[count_left:]
+        swapped = pltpu.roll(imaginary, half, axis=1)
+        wheres = lax.broadcasted_iota(jnp.int32, swapped.shape, 1)
+        combined = real + jnp.where(wheres < half, swapped, -swapped)
+        partial[pl.ds(pl.multiple_of(chunk * count_left, count_left), count_left), :] = combined
+
+    def step_chunk(step, carry):
+        @pl.when(step < chunks)
+        def _():
+            stage(step)
+
+        @pl.when(step > 0)
+        def _():
+            compute(step - 1)
+
+        return carry
+
+    lax.fori_loop(0, chunks + 1, step_chunk, 0)
+
+    share_rows = shares.shape[1]
+
+    def rows_of(site):
+        return pl.ds(pl.multiple_of(site * share_rows, share_rows), share_rows)
+
+    def share_copy(step):
+        site = lax.rem(my_site + step, sites)
+        return pltpu.make_async_remote_copy(
+            src_ref=partial.at[rows_of(site)],
+            dst_ref=shares.at[my_site],
+            send_sem=share_send.at[step],
+            recv_sem=share_recv,
+            device_id={"sites": site},
+            device_id_type=MESH,
+        )
+
+    def total_copy(step):
+        site = lax.rem(my_site + step, sites)
+        return pltpu.make_async_remote_copy(
+            src_ref=total.at[rows_of(my_site)],
+            dst_ref=total.at[rows_of(my_site)],
+            send_sem=total_send.at[step],
+            recv_sem=total_recv,
+            device_id={"sites": site},
+            device_id_type=MESH,
+        )
+
+    def start_all(make, stop):
+        def go(step, carry):
+            make(step).start()
+            return carry
+
+        lax.fori_loop(1, stop, go, 0)
+
+    def sent_all(make, stop):
+        def go(step, carry):
+            make(step).wait_send()
+            return carry
+
+        lax.fori_loop(1, stop, go, 0)
+
+    start_all(share_copy, sites)
+    pltpu.make_async_copy(partial.at[rows_of(my_site)], shares.at[my_site], share_recv).start()
+    pltpu.make_async_copy(shares, shares, share_recv).wait()
+    summed = shares[0]
+    for site in range(1, sites):
+        summed = summed + shares[site]
+    total[rows_of(my_site), :] = summed
+    start_all(total_copy, sites)
+    whole = total.at[pl.ds(0, (sites - 1) * share_rows)]
+    pltpu.make_async_copy(whole, whole, total_recv).wait()
+    out_ref[...] = total[...]
+    sent_all(share_copy, sites)
+    sent_all(total_copy, sites)
+
+    def sent_chunk(chunk, carry):
+        sent_all(functools.partial(piece_copy, chunk), count)
+        return carry
+
+    lax.fori_loop(0, chunks, sent_chunk, 0)
+
+
+def per_device_fused(groups, sites, right_vectors, left_vectors, vacancy):
+    width_group = right_vectors.shape[1]
+    count_left, rows, width = left_vectors.shape[1:]
+    wide = COLS_AT_ONCE
+    chunks = width_group // wide
+    padded = rows + 2 * HALO
+    field = pltpu.VMEM((padded, 2, wide, width), jnp.float32)
+    mask = pltpu.VMEM((padded, 8, width), jnp.float32)
+    sums = (chunks * count_left, 2 * MOM * wide)
+    dma = pltpu.SemaphoreType.DMA
+    call = pl.pallas_call(
+        functools.partial(fused_kernel, groups, sites),
+        out_shape=jax.ShapeDtypeStruct(sums, jnp.float32),
+        in_specs=[
+            pl.BlockSpec(memory_space=pl.ANY),
+            pl.BlockSpec(memory_space=pltpu.VMEM),
+            pl.BlockSpec(memory_space=pltpu.VMEM),
+        ],
+        out_specs=pl.BlockSpec(memory_space=pltpu.VMEM),
+        scratch_shapes=[
+            pltpu.VMEM((chunks, padded, 2, wide, width), jnp.float32),
+            field, field, field, field, mask, mask, mask,
+            pltpu.VMEM((2 * MOM * wide, padded * width), jnp.bfloat16),
+            pltpu.VMEM(sums, jnp.float32),
+            pltpu.VMEM((sites, sums[0] // sites, sums[1]), jnp.float32),
+            pltpu.VMEM(sums, jnp.float32),
+            dma((chunks, groups * sites)), dma((chunks,)),
+            dma((chunks, 2)), dma((chunks, 2)), dma((2,)), dma((2,)),
+            dma((sites,)), dma, dma((sites,)), dma,
+        ],
+        compiler_params=pltpu.CompilerParams(
+            collective_id=0, has_side_effects=True, vmem_limit_bytes=48 * 1024 * 1024
+        ),
+        cost_estimate=pl.CostEstimate(flops=2 * 10**9, bytes_accessed=8 * 10**6, transcendentals=0),
+    )
+    summed = call(right_vectors, left_vectors.reshape(2 * count_left, rows * width), vacancy)
+    summed = summed.reshape(chunks, count_left, 2, MOM, wide)
+    return summed.transpose(2, 3, 1, 0, 4).reshape(2, MOM, count_left, width_group, 1)
+
+
+def per_device(groups, sites, right_vectors, left_vectors, vacancy):
+    columns, piece = right_vectors.shape[1], right_vectors.shape[5]
+    count_left, rows, width = left_vectors.shape[1:]
+    shares = (columns // COLS_AT_ONCE) * count_left
+    fits = (
+        piece % 128 == 0 and width % piece == 0 and right_vectors.shape[4] == 1
+        and columns % COLS_AT_ONCE == 0 and rows % 2 == 0 and rows >= HALO
+        and sites >= 3 and shares % (8 * sites) == 0 and count_left % 8 == 0
+    )
+    if fits:
+        return per_device_fused(groups, sites, right_vectors, left_vectors, vacancy)
+    return per_device_plain(right_vectors, left_vectors, vacancy)
+
+
 def solution(mesh):
     return jax.shard_map(
-        per_device,
+        functools.partial(per_device, mesh.shape["cols"], mesh.shape["sites"]),
         mesh=mesh,
         in_specs=(
             P(None, None, None, None, ("cols", "sites"), None),

time: 477 us -> 164 us (0.34); the launches traced: 468 us -> 164 us
  waiting for transfers between devices: 187 us -> 0 us
  Pallas kernels: 0 us -> 160 us
  other arithmetic: 130 us -> 0 us
  local copies, waits for them, and re-layouts: 56.5 us -> 4.09 us
  blocking collectives: 51.5 us -> 0 us
  starting transfers between devices: 26.5 us -> 0 us
  between operations: 13.9 us -> 0.04 us
    pallas_call x0 -> x1, Pallas kernels: none -> 160 us  [per_device_fused(): call(right_vectors, left_vectors.reshape(2 * count_left, rows * width), v...]
    psum x1 -> x0, waiting for transfers between devices: 85.7 us -> none  [per_device(): summed_list.append(lax.psum(combined, 'sites'))]
    all_to_all x1 -> x0, waiting for transfers between devices: 74.5 us -> none  [per_device(): lax.all_to_all(lax.all_to_all(pieces, 'cols', split_axis=2, concat_axis=2...]
    all_to_all x1 -> x0, blocking collectives: 51.5 us -> none  [per_device(): lax.all_to_all(pieces, 'cols', split_axis=2, concat_axis=2, tiled=True)]
    slice x4 -> x0, other arithmetic: 47.3 us -> none  [column_shift(): return jnp.concatenate([values[..., offset:], filler], axis=-1)]
    convert_element_type x5 -> x0, other arithmetic: 31.3 us -> none  [the longest x4 31.3 us: per_device(): rounded = moment.astype(jnp.bfloat16).reshape(2 * group_width, site_count)]
    sub x7 -> x0, other arithmetic: 28.1 us -> none  [the longest x3 28 us: haldane(): column_shift(centre, 2) - column_shift(centre, -2)]
    ppermute x8 -> x0, waiting for transfers between devices: 26.5 us -> none  [the longest x4 17.2 us: padded_2(): lax.ppermute(tail, axis, [(i, (i + 1) % count) for i in range(count)])]
  transfers between devices with their start and end apart: 10 -> 0, of which waited for: 9 -> 0; matrix products, arithmetic and copies ran while one was open for 2% -> 0% of each run, Pallas kernels for 0% -> 0%
where the time goes in v1:
time: 164 us
  Pallas kernels  160 us (98%)
  local copies, waits for them, and re-layouts  4.09 us (2%)
    pallas_call x1, Pallas kernels, per_device_fused(): call(right_vectors, left_vectors.reshape(2 * count_left, rows * width), v...  160 us

profile of v1, /device:TPU:0, one launch (start us, length us, event | category | flops | bytes accessed | tf_op | source)
XLA Modules:
  0.0 164.3 jit_solution(10370019405252445423)
XLA Ops:
  0.0 0.0 copy-start
  0.0 3.0 %copy.8 = bf16[16,8,16,512]{3,1,2,0:T(8,128)(2,1)S(1)} copy(bf16[16,8,16,512]{3,2,1,0:T(8,128)(2,1)} %bitcast.8) | data formatting | bytes 4194304
  3.0 0.0 copy-done
  3.0 160.2 %shard_map.37 = f32[256,128]{1,0:T(8,128)S(1)} custom-call(f32[2,64,2,16,1,256]{5,4,3,2,1,0:T(1,128)} %right_ref.1, bf16[128,8192]{1,0:T(8,128)(2,1)S(1)} %bitcast.7, s32[16,512]{1,0:T(8,128)S(1)} %copy-done), custom_call_target="tpu_custom_call" | custom-call | flops 2000000000 | bytes 8000000 | tf_op jit(solution)/shard_map/pallas_call | solution.py:441
  163.2 0.1 copy.5
  163.3 0.2 reshape.10
  163.4 0.8 copy.7
  (1 shorter events, 0.0 us)
Async XLA Ops:
  0.0 3.0 %copy-start = (s32[16,512]{1,0:T(8,128)S(1)}, s32[16,512]{1,0:T(8,128)}, u32[]{:S(2)}) copy-start(s32[16,512]{1,0:T(8,128)} %vacancy_ref.1) | copy-start | bytes 98308

commit v2 on v1

--- a/solution.py
+++ b/solution.py
@@ -223,7 +223,7 @@
         pltpu.make_async_copy(piece_of(chunk, my_group, my_site), landing(chunk, mine), piece_recv.at[chunk]).start()
         return carry
 
-    lax.fori_loop(0, chunks, send_chunk, 0)
+    lax.fori_loop(0, min(2, chunks), send_chunk, 0)
 
     for copy in mask_copies():
         copy.wait()
@@ -298,6 +298,10 @@
         for copy in rim_copies(chunk):
             copy.start()
 
+        @pl.when(chunk + 2 < chunks)
+        def _():
+            send_chunk(chunk + 2, 0)
+
     def compute(chunk):
         for copy in rim_copies(chunk):
             copy.wait()

time: 164 us -> 150 us (0.915)
  Pallas kernels: 160 us -> 146 us
    pallas_call x1, Pallas kernels: 160 us -> 146 us  [per_device_fused(): call(right_vectors, left_vectors.reshape(2 * count_left, rows * width), v...]
where the time goes in v2:
time: 150 us
  Pallas kernels  146 us (97%)
  local copies, waits for them, and re-layouts  4.09 us (3%)
    pallas_call x1, Pallas kernels, per_device_fused(): call(right_vectors, left_vectors.reshape(2 * count_left, rows * width), v...  146 us

profile of v2, /device:TPU:0, one launch (start us, length us, event | category | flops | bytes accessed | tf_op | source)
XLA Modules:
  0.0 149.6 jit_solution(4145340655276077608)
XLA Ops:
  0.0 0.0 copy-start
  0.0 3.0 %copy.8 = bf16[16,8,16,512]{3,1,2,0:T(8,128)(2,1)S(1)} copy(bf16[16,8,16,512]{3,2,1,0:T(8,128)(2,1)} %bitcast.8) | data formatting | bytes 4194304
  3.0 0.0 copy-done
  3.0 145.5 %shard_map.37 = f32[256,128]{1,0:T(8,128)S(1)} custom-call(f32[2,64,2,16,1,256]{5,4,3,2,1,0:T(1,128)} %right_ref.1, bf16[128,8192]{1,0:T(8,128)(2,1)S(1)} %bitcast.7, s32[16,512]{1,0:T(8,128)S(1)} %copy-done), custom_call_target="tpu_custom_call" | custom-call | flops 2000000000 | bytes 8000000 | tf_op jit(solution)/shard_map/pallas_call | solution.py:445
  148.5 0.1 copy.5
  148.6 0.2 reshape.10
  148.8 0.8 copy.7
  (1 shorter events, 0.0 us)
Async XLA Ops:
  0.0 3.0 %copy-start = (s32[16,512]{1,0:T(8,128)S(1)}, s32[16,512]{1,0:T(8,128)}, u32[]{:S(2)}) copy-start(s32[16,512]{1,0:T(8,128)} %vacancy_ref.1) | copy-start | bytes 98308

commit v3 on v2

--- a/solution.py
+++ b/solution.py
@@ -179,8 +179,9 @@
         return right_ref.at[:, pl.ds(pl.multiple_of(chunk * wide, wide), wide), group, site, 0, :]
 
     def piece_copy(chunk, step):
-        other = lax.rem(mine + step, count)
-        group, site = other // sites, lax.rem(other, sites)
+        turn = lax.rem(step, 2) * (sites // 2) + step // (2 * groups)
+        group = lax.rem(my_group + lax.rem(step // 2, groups), groups)
+        site = lax.rem(my_site + turn, sites)
         return pltpu.make_async_remote_copy(
             src_ref=piece_of(chunk, group, site),
             dst_ref=landing(chunk, mine),
@@ -454,7 +455,7 @@
     fits = (
         piece % 128 == 0 and width % piece == 0 and right_vectors.shape[4] == 1
         and columns % COLS_AT_ONCE == 0 and rows % 2 == 0 and rows >= HALO
-        and sites >= 3 and shares % (8 * sites) == 0 and count_left % 8 == 0
+        and sites >= 4 and sites % 2 == 0 and shares % (8 * sites) == 0 and count_left % 8 == 0
     )
     if fits:
         return per_device_fused(groups, sites, right_vectors, left_vectors, vacancy)

time: 150 us -> 149 us (level)
  no operation moved by 1% of the time
where the time goes in v3:
time: 149 us
  Pallas kernels  145 us (97%)
  local copies, waits for them, and re-layouts  4.09 us (3%)
    pallas_call x1, Pallas kernels, per_device_fused(): call(right_vectors, left_vectors.reshape(2 * count_left, rows * width), v...  145 us
    unnamed x3, local copies, waits for them, and re-layouts  2.98 us

profile of v3, /device:TPU:0, one launch (start us, length us, event | category | flops | bytes accessed | tf_op | source)
XLA Modules:
  0.0 148.8 jit_solution(6470669150535281523)
XLA Ops:
  0.0 0.0 copy-start
  0.0 3.0 %copy.8 = bf16[16,8,16,512]{3,1,2,0:T(8,128)(2,1)S(1)} copy(bf16[16,8,16,512]{3,2,1,0:T(8,128)(2,1)} %bitcast.8) | data formatting | bytes 4194304
  3.0 0.0 copy-done
  3.0 144.7 %shard_map.37 = f32[256,128]{1,0:T(8,128)S(1)} custom-call(f32[2,64,2,16,1,256]{5,4,3,2,1,0:T(1,128)} %right_ref.1, bf16[128,8192]{1,0:T(8,128)(2,1)S(1)} %bitcast.7, s32[16,512]{1,0:T(8,128)S(1)} %copy-done), custom_call_target="tpu_custom_call" | custom-call | flops 2000000000 | bytes 8000000 | tf_op jit(solution)/shard_map/pallas_call | solution.py:446
  147.7 0.1 copy.5
  147.8 0.2 reshape.10
  148.0 0.8 copy.7
  (1 shorter events, 0.0 us)
Async XLA Ops:
  0.0 3.0 %copy-start = (s32[16,512]{1,0:T(8,128)S(1)}, s32[16,512]{1,0:T(8,128)}, u32[]{:S(2)}) copy-start(s32[16,512]{1,0:T(8,128)} %vacancy_ref.1) | copy-start | bytes 98308

commit v4 on v3

--- a/solution.py
+++ b/solution.py
@@ -133,14 +133,15 @@
 MESH = pl.DeviceIdType.MESH
 HALO = MOM
 COLS_AT_ONCE = 16
+LANES = 128
 
 
 def fused_kernel(
     groups, sites, right_ref, left_ref, vacancy_ref, out_ref,
     arrived, field0, field1, field2, field3, present, scaled, doubled, rounded,
-    partial, shares, total,
+    left_held, left_wide, left_flat, partial, shares, total,
     piece_send, piece_recv, rim_send, rim_recv, mask_send, mask_recv,
-    share_send, share_recv, total_send, total_recv,
+    share_send, share_recv, total_send, total_recv, left_sem,
 ):
     chunks, padded_rows, _, wide, width = arrived.shape
     rows = padded_rows - 2 * HALO
@@ -151,6 +152,8 @@
     mine = my_group * sites + my_site
     above, below = lax.rem(my_site + 1, sites), lax.rem(my_site + sites - 1, sites)
 
+    left_copy = pltpu.make_async_copy(left_ref, left_held, left_sem)
+    left_copy.start()
     barrier = pltpu.get_barrier_semaphore()
 
     def greet(step, carry):
@@ -161,9 +164,6 @@
         return carry
 
     lax.fori_loop(1, count, greet, 0)
-
-    lane = lax.broadcasted_iota(jnp.int32, (8, width), 1)
-    odd_lane = lax.rem(lane, 2) == 1
 
     for row in range(rows):
         present[HALO + row] = jnp.broadcast_to(vacancy_ref[row : row + 1, :].astype(jnp.float32), (8, width))
@@ -237,54 +237,74 @@
 
     lax.fori_loop(0, padded_rows, scale_masks, 0)
 
+    tiles = [slice(at, at + LANES) for at in range(0, width, LANES)]
+    lane = lax.broadcasted_iota(jnp.int32, (8, LANES), 1)
+    odd_lane = lax.rem(lane, 2) == 1
+    even_sign = jnp.where(odd_lane, -1.0, 1.0)
+    nothing = jnp.zeros((8, LANES), jnp.float32)
+
     def shift(values, offset):
-        turned = pltpu.roll(values, width - 1 if offset > 0 else 1, axis=1)
-        return jnp.where(lane == (width - 1 if offset > 0 else 0), 0.0, turned)
-
-    def signed(values, odd_row):
-        return jnp.where(odd_lane != odd_row, -values, values)
+        if offset > 0:
+            turned = [pltpu.roll(v, LANES - 1, axis=1) for v in values]
+            return [jnp.where(lane == LANES - 1, b, a) for a, b in zip(turned, turned[1:] + [nothing])]
+        turned = [pltpu.roll(v, 1, axis=1) for v in values]
+        return [jnp.where(lane == 0, b, a) for a, b in zip(turned, [nothing] + turned[:-1])]
 
     def sweep(source, target, earlier, mask, degree):
         first = degree + 1
 
         def one_row(row, odd_row):
+            sign = -even_sign if odd_row else even_sign
+            second, onsite = SECOND_HOP * sign, ONSITE_MASS * sign
+            down = odd_lane != odd_row
+            factor = [mask[row, :, at] for at in tiles]
             halves = [[], []]
             for part in range(0, wide, 8):
-                at = slice(part, part + 8)
-                centre = [source[row, r, at, :] for r in (0, 1)]
-                upper = [source[row + 1, r, at, :] for r in (0, 1)]
-                lower = [source[row - 1, r, at, :] for r in (0, 1)]
-                right = [shift(c, 1) for c in centre]
-                left = [shift(c, -1) for c in centre]
-                both = [u + l for u, l in zip(upper, lower)]
+                eight = slice(part, part + 8)
+                far, rest = [], []
+                for r in (0, 1):
+                    centre = [source[row, r, eight, at] for at in tiles]
+                    upper = [source[row + 1, r, eight, at] for at in tiles]
+                    lower = [source[row - 1, r, eight, at] for at in tiles]
+                    right, left = shift(centre, 1), shift(centre, -1)
+                    both = [u + l for u, l in zip(upper, lower)]
+                    if degree == 0:
+                        ahead = shift([2.0 * v - w for v, w in zip(right, both)], 1)
+                        behind = shift([2.0 * v - w for v, w in zip(left, both)], -1)
+                        far.append([second * (v + w) for v, w in zip(ahead, behind)])
+                        rest.append([v - w for v, w in zip(right, left)])
+                    else:
+                        ahead = shift([v - w for v, w in zip(right, both)], 1)
+                        behind = shift([v - w for v, w in zip(left, both)], -1)
+                        far.append([second * (v - w) for v, w in zip(ahead, behind)])
+                        rest.append([
+                            (onsite * c + jnp.where(down, l, u)) + (v + w)
+                            for c, u, l, v, w in zip(centre, upper, lower, right, left)
+                        ])
                 if degree == 0:
-                    far = [shift(2.0 * a - s, 1) + shift(2.0 * b - s, -1) for a, b, s in zip(right, left, both)]
-                    near = [a - b for a, b in zip(right, left)]
                     applied = [
-                        -near[1] - signed(SECOND_HOP * far[0], odd_row),
-                        near[0] - signed(SECOND_HOP * far[1], odd_row),
+                        [-v - w for v, w in zip(rest[1], far[0])],
+                        [v - w for v, w in zip(rest[0], far[1])],
                     ]
                 else:
-                    far = [shift(a - s, 1) - shift(b - s, -1) for a, b, s in zip(right, left, both)]
-                    phase = [-far[1], far[0]]
                     applied = [
-                        signed(ONSITE_MASS * centre[r] + SECOND_HOP * phase[r], odd_row)
-                        + (right[r] + left[r])
-                        + jnp.where(odd_lane != odd_row, lower[r], upper[r])
-                        for r in (0, 1)
+                        [v - w for v, w in zip(rest[0], far[1])],
+                        [v + w for v, w in zip(rest[1], far[0])],
                     ]
-                factor = mask[row]
                 for r in (0, 1):
-                    result = applied[r] * factor
+                    results = [v * f for v, f in zip(applied[r], factor)]
                     if earlier is not None:
-                        result = result - earlier[row, r, at, :]
+                        results = [v - earlier[row, r, eight, at] for v, at in zip(results, tiles)]
                     if target is not None:
-                        target[row, r, at, :] = result
-                    halves[r].append(result)
-            lanes = pl.ds(pl.multiple_of(row * width, width), width)
+                        for v, at in zip(results, tiles):
+                            target[row, r, eight, at] = v
+                    halves[r].append(results)
             for r in (0, 1):
                 base = (r * MOM + degree) * wide
-                rounded[base : base + wide, lanes] = jnp.concatenate(halves[r], axis=0).astype(jnp.bfloat16)
+                for i, at in enumerate(tiles):
+                    lanes = pl.ds(pl.multiple_of(row * width + at.start, LANES), LANES)
+                    block = jnp.concatenate([half[i] for half in halves[r]], axis=0)
+                    rounded[base : base + wide, lanes] = block.astype(jnp.bfloat16)
 
         def pair(step, carry):
             one_row(first + 2 * step, first % 2 == 1)
@@ -292,6 +312,22 @@
             return carry
 
         lax.fori_loop(0, (padded_rows - 2 * first) // 2, pair, 0)
+
+    left_copy.wait()
+
+    def widen(step, carry):
+        at = pl.ds(pl.multiple_of(step * 16, 16), 16)
+        block = left_held[at, :].astype(jnp.float32)
+        for i, lanes in enumerate(tiles):
+            left_wide[i, at, :] = block[:, lanes]
+        return carry
+
+    lax.fori_loop(0, left_ref.shape[0] // 16, widen, 0)
+    left_count = left_ref.shape[0] // rows
+    for row in range(rows):
+        for i, lanes in enumerate(tiles):
+            block = left_wide[i, pl.ds(row, left_count, stride=rows), :]
+            left_flat[:, row * width + lanes.start : row * width + lanes.stop] = block.astype(jnp.bfloat16)
 
     def stage(chunk):
         held = arrived.at[chunk, pl.ds(HALO, rows)]
@@ -320,7 +356,7 @@
         sweep(field2, field3, field1, doubled, 2)
         sweep(field3, None, field2, doubled, 3)
         product = lax.dot_general(
-            left_ref[...],
+            left_flat[...],
             rounded[:, HALO * width : (HALO + rows) * width],
             (((1,), (1,)), ((), ())),
             preferred_element_type=jnp.float32,
@@ -423,7 +459,7 @@
         out_shape=jax.ShapeDtypeStruct(sums, jnp.float32),
         in_specs=[
             pl.BlockSpec(memory_space=pl.ANY),
-            pl.BlockSpec(memory_space=pltpu.VMEM),
+            pl.BlockSpec(memory_space=pl.ANY),
             pl.BlockSpec(memory_space=pltpu.VMEM),
         ],
         out_specs=pl.BlockSpec(memory_space=pltpu.VMEM),
@@ -431,19 +467,22 @@
             pltpu.VMEM((chunks, padded, 2, wide, width), jnp.float32),
             field, field, field, field, mask, mask, mask,
             pltpu.VMEM((2 * MOM * wide, padded * width), jnp.bfloat16),
+            pltpu.VMEM((2 * count_left * rows, width), jnp.bfloat16),
+            pltpu.VMEM((width // LANES, 2 * count_left * rows, LANES), jnp.float32),
+            pltpu.VMEM((2 * count_left, rows * width), jnp.bfloat16),
             pltpu.VMEM(sums, jnp.float32),
             pltpu.VMEM((sites, sums[0] // sites, sums[1]), jnp.float32),
             pltpu.VMEM(sums, jnp.float32),
             dma((chunks, groups * sites)), dma((chunks,)),
             dma((chunks, 2)), dma((chunks, 2)), dma((2,)), dma((2,)),
-            dma((sites,)), dma, dma((sites,)), dma,
+            dma((sites,)), dma, dma((sites,)), dma, dma,
         ],
         compiler_params=pltpu.CompilerParams(
             collective_id=0, has_side_effects=True, vmem_limit_bytes=48 * 1024 * 1024
         ),
         cost_estimate=pl.CostEstimate(flops=2 * 10**9, bytes_accessed=8 * 10**6, transcendentals=0),
     )
-    summed = call(right_vectors, left_vectors.reshape(2 * count_left, rows * width), vacancy)
+    summed = call(right_vectors, left_vectors.reshape(2 * count_left * rows, width), vacancy)
     summed = summed.reshape(chunks, count_left, 2, MOM, wide)
     return summed.transpose(2, 3, 1, 0, 4).reshape(2, MOM, count_left, width_group, 1)
 
@@ -455,7 +494,7 @@
     fits = (
         piece % 128 == 0 and width % piece == 0 and right_vectors.shape[4] == 1
         and columns % COLS_AT_ONCE == 0 and rows % 2 == 0 and rows >= HALO
-        and sites >= 4 and sites % 2 == 0 and shares % (8 * sites) == 0 and count_left % 8 == 0
+        and sites >= 4 and sites % 2 == 0 and shares % (8 * sites) == 0 and count_left % 8 == 0 and (2 * count_left * rows) % 16 == 0
     )
     if fits:
         return per_device_fused(groups, sites, right_vectors, left_vectors, vacancy)

time: 149 us -> 147 us (0.987)
    unnamed x3 -> x4, local copies, waits for them, and re-layouts: 2.98 us -> 2.35 us
where the time goes in v4:
time: 147 us
  Pallas kernels  144 us (98%)
  local copies, waits for them, and re-layouts  3.45 us (2%)
    pallas_call x1, Pallas kernels, per_device_fused(): call(right_vectors, left_vectors.reshape(2 * count_left * rows, width), v...  144 us

profile of v4, /device:TPU:0, one launch (start us, length us, event | category | flops | bytes accessed | tf_op | source)
XLA Modules:
  0.0 147.3 jit_solution(17129048097869250725)
XLA Ops:
  0.0 0.0 copy-start
  0.0 1.6 %copy-done = bf16[2,64,16,512]{3,2,1,0:T(8,128)(2,1)S(1)} copy-done((bf16[2,64,16,512]{3,2,1,0:T(8,128)(2,1)S(1)}, bf16[2,64,16,512]{3,2,1,0:T(8,128)(2,1)}, u32[]{:S(2)}) %copy-start) | copy-done | bytes 2097176
  1.6 0.0 copy-start.1
  1.6 0.8 copy-done.1
  2.4 143.8 %shard_map.37 = f32[256,128]{1,0:T(8,128)S(1)} custom-call(f32[2,64,2,16,1,256]{5,4,3,2,1,0:T(1,128)} %right_ref.1, bf16[2048,512]{1,0:T(8,128)(2,1)S(1)} %bitcast.5, s32[16,512]{1,0:T(8,128)S(1)} %copy-done.1), custom_call_target="tpu_custom_call" | custom-call | flops 2000000000 | bytes 8000000 | tf_op jit(solution)/shard_map/pallas_call | solution.py:485
  146.1 0.1 copy.5
  146.3 0.2 reshape.10
  146.4 0.8 copy.7
  (1 shorter events, 0.0 us)
Async XLA Ops:
  0.0 1.6 %copy-start = (bf16[2,64,16,512]{3,2,1,0:T(8,128)(2,1)S(1)}, bf16[2,64,16,512]{3,2,1,0:T(8,128)(2,1)}, u32[]{:S(2)}) copy-start(bf16[2,64,16,512]{3,2,1,0:T(8,128)(2,1)} %param.4) | copy-start | bytes 6291460
  1.6 0.8 copy-start.1

commit v5 on v4

--- a/solution.py
+++ b/solution.py
@@ -139,19 +139,31 @@
 def fused_kernel(
     groups, sites, right_ref, left_ref, vacancy_ref, out_ref,
     arrived, field0, field1, field2, field3, present, scaled, doubled, rounded,
-    left_held, left_wide, left_flat, partial, shares, total,
+    staged, left_held, left_wide, left_flat, partial, shares, total,
     piece_send, piece_recv, rim_send, rim_recv, mask_send, mask_recv,
-    share_send, share_recv, total_send, total_recv, left_sem,
+    share_send, share_recv, total_send, total_recv, left_sem, stage_sem,
 ):
-    chunks, padded_rows, _, wide, width = arrived.shape
+    chunks, padded_rows, per_row, _, wide, piece = arrived.shape
+    width = per_row * piece
     rows = padded_rows - 2 * HALO
-    piece = right_ref.shape[5]
-    per_row = width // piece
     count = groups * sites
     my_group, my_site = lax.axis_index("cols"), lax.axis_index("sites")
     mine = my_group * sites + my_site
     above, below = lax.rem(my_site + 1, sites), lax.rem(my_site + sites - 1, sites)
 
+    def piece_of(chunk, group, site):
+        return right_ref.at[:, pl.ds(pl.multiple_of(chunk * wide, wide), wide), group, site, 0, :]
+
+    def lay_out(chunk, carry):
+        def place(other, inner):
+            pltpu.make_async_copy(
+                piece_of(chunk, other // sites, lax.rem(other, sites)), staged.at[chunk, other], stage_sem.at[chunk]
+            ).start()
+            return inner
+
+        lax.fori_loop(0, count, place, 0)
+        return carry
+
     left_copy = pltpu.make_async_copy(left_ref, left_held, left_sem)
     left_copy.start()
     barrier = pltpu.get_barrier_semaphore()
@@ -164,6 +176,7 @@
         return carry
 
     lax.fori_loop(1, count, greet, 0)
+    lay_out(0, 0)
 
     for row in range(rows):
         present[HALO + row] = jnp.broadcast_to(vacancy_ref[row : row + 1, :].astype(jnp.float32), (8, width))
@@ -171,19 +184,14 @@
     pl.semaphore_wait(barrier, count - 1)
 
     def landing(chunk, run):
-        return arrived.at[
-            chunk, HALO + run // per_row, :, :, pl.ds(pl.multiple_of(lax.rem(run, per_row) * piece, piece), piece)
-        ]
-
-    def piece_of(chunk, group, site):
-        return right_ref.at[:, pl.ds(pl.multiple_of(chunk * wide, wide), wide), group, site, 0, :]
+        return arrived.at[chunk, HALO + run // per_row, lax.rem(run, per_row)]
 
     def piece_copy(chunk, step):
         turn = lax.rem(step, 2) * (sites // 2) + step // (2 * groups)
         group = lax.rem(my_group + lax.rem(step // 2, groups), groups)
         site = lax.rem(my_site + turn, sites)
         return pltpu.make_async_remote_copy(
-            src_ref=piece_of(chunk, group, site),
+            src_ref=staged.at[chunk, group * sites + site],
             dst_ref=landing(chunk, mine),
             send_sem=piece_send.at[chunk, step],
             recv_sem=piece_recv.at[chunk],
@@ -216,15 +224,19 @@
         copy.start()
 
     def send_chunk(chunk, carry):
+        pltpu.make_async_copy(staged.at[chunk], staged.at[chunk], stage_sem.at[chunk]).wait()
+
         def send(step, inner):
             piece_copy(chunk, step).start()
             return inner
 
         lax.fori_loop(1, count, send, 0)
-        pltpu.make_async_copy(piece_of(chunk, my_group, my_site), landing(chunk, mine), piece_recv.at[chunk]).start()
-        return carry
-
-    lax.fori_loop(0, min(2, chunks), send_chunk, 0)
+        pltpu.make_async_copy(staged.at[chunk, mine], landing(chunk, mine), piece_recv.at[chunk]).start()
+        return carry
+
+    send_chunk(0, 0)
+    lax.fori_loop(1, chunks, lay_out, 0)
+    lax.fori_loop(1, min(2, chunks), send_chunk, 0)
 
     for copy in mask_copies():
         copy.wait()
@@ -347,7 +359,9 @@
             for r in (0, 1):
                 for part in range(0, wide, 8):
                     at = slice(part, part + 8)
-                    field0[row, r, at, :] = arrived[chunk, row, r, at, :] * present[row]
+                    for run in range(per_row):
+                        lanes = slice(run * piece, (run + 1) * piece)
+                        field0[row, r, at, lanes] = arrived[chunk, row, run, r, at, :] * present[row, :, lanes]
             return carry
 
         lax.fori_loop(0, padded_rows, mask_row, 0)
@@ -445,7 +459,7 @@
 
 
 def per_device_fused(groups, sites, right_vectors, left_vectors, vacancy):
-    width_group = right_vectors.shape[1]
+    width_group, piece = right_vectors.shape[1], right_vectors.shape[5]
     count_left, rows, width = left_vectors.shape[1:]
     wide = COLS_AT_ONCE
     chunks = width_group // wide
@@ -458,15 +472,16 @@
         functools.partial(fused_kernel, groups, sites),
         out_shape=jax.ShapeDtypeStruct(sums, jnp.float32),
         in_specs=[
-            pl.BlockSpec(memory_space=pl.ANY),
-            pl.BlockSpec(memory_space=pl.ANY),
+            pl.BlockSpec(memory_space=pltpu.HBM),
+            pl.BlockSpec(memory_space=pltpu.HBM),
             pl.BlockSpec(memory_space=pltpu.VMEM),
         ],
         out_specs=pl.BlockSpec(memory_space=pltpu.VMEM),
         scratch_shapes=[
-            pltpu.VMEM((chunks, padded, 2, wide, width), jnp.float32),
+            pltpu.VMEM((chunks, padded, width // piece, 2, wide, piece), jnp.float32),
             field, field, field, field, mask, mask, mask,
             pltpu.VMEM((2 * MOM * wide, padded * width), jnp.bfloat16),
+            pltpu.VMEM((chunks, groups * sites, 2, wide, piece), jnp.float32),
             pltpu.VMEM((2 * count_left * rows, width), jnp.bfloat16),
             pltpu.VMEM((width // LANES, 2 * count_left * rows, LANES), jnp.float32),
             pltpu.VMEM((2 * count_left, rows * width), jnp.bfloat16),
@@ -475,10 +490,10 @@
             pltpu.VMEM(sums, jnp.float32),
             dma((chunks, groups * sites)), dma((chunks,)),
             dma((chunks, 2)), dma((chunks, 2)), dma((2,)), dma((2,)),
-            dma((sites,)), dma, dma((sites,)), dma, dma,
+            dma((sites,)), dma, dma((sites,)), dma, dma, dma((chunks,)),
         ],
         compiler_params=pltpu.CompilerParams(
-            collective_id=0, has_side_effects=True, vmem_limit_bytes=48 * 1024 * 1024
+            collective_id=0, has_side_effects=True, vmem_limit_bytes=125 * 512 * 1024
         ),
         cost_estimate=pl.CostEstimate(flops=2 * 10**9, bytes_accessed=8 * 10**6, transcendentals=0),
     )

time: 147 us -> 147 us (level)
    unnamed x4 -> x0, local copies, waits for them, and re-layouts: 2.35 us -> none
where the time goes in v5:
time: 147 us
  Pallas kernels  145 us (99%)
  local copies, waits for them, and re-layouts  2.01 us (1%)
    pallas_call x1, Pallas kernels, per_device_fused(): call(right_vectors, left_vectors.reshape(2 * count_left * rows, width), v...  145 us

profile of v5, /device:TPU:0, one launch (start us, length us, event | category | flops | bytes accessed | tf_op | source)
XLA Modules:
  0.0 146.8 jit_solution(17090965490362514740)
XLA Ops:
  0.0 144.8 %shard_map.37 = f32[256,128]{1,0:T(8,128)} custom-call(f32[2,64,2,16,1,256]{5,4,3,2,1,0:T(1,128)} %right_ref.1, bf16[2048,512]{1,0:T(8,128)(2,1)} %bitcast.7, s32[16,512]{1,0:T(8,128)} %vacancy_ref.1), custom_call_target="tpu_custom_call" | custom-call | flops 2000000000 | bytes 8000000 | tf_op jit(solution)/shard_map/pallas_call | solution.py:500
  144.8 1.0 copy.5
  145.8 0.2 reshape.10
  146.0 0.8 copy.7
  (1 shorter events, 0.0 us)

commit v6 on v5

--- a/solution.py
+++ b/solution.py
@@ -227,6 +227,10 @@
         pltpu.make_async_copy(staged.at[chunk], staged.at[chunk], stage_sem.at[chunk]).wait()
 
         def send(step, inner):
+            @pl.when(chunk > 0)
+            def _():
+                piece_copy(chunk - 1, step).wait_send()
+
             piece_copy(chunk, step).start()
             return inner
 
@@ -236,7 +240,6 @@
 
     send_chunk(0, 0)
     lax.fori_loop(1, chunks, lay_out, 0)
-    lax.fori_loop(1, min(2, chunks), send_chunk, 0)
 
     for copy in mask_copies():
         copy.wait()
@@ -347,10 +350,6 @@
         for copy in rim_copies(chunk):
             copy.start()
 
-        @pl.when(chunk + 2 < chunks)
-        def _():
-            send_chunk(chunk + 2, 0)
-
     def compute(chunk):
         for copy in rim_copies(chunk):
             copy.wait()
@@ -383,18 +382,16 @@
         combined = real + jnp.where(wheres < half, swapped, -swapped)
         partial[pl.ds(pl.multiple_of(chunk * count_left, count_left), count_left), :] = combined
 
-    def step_chunk(step, carry):
-        @pl.when(step < chunks)
+    def step_chunk(chunk, carry):
+        @pl.when(chunk + 1 < chunks)
         def _():
-            stage(step)
-
-        @pl.when(step > 0)
-        def _():
-            compute(step - 1)
-
+            send_chunk(chunk + 1, 0)
+
+        stage(chunk)
+        compute(chunk)
         return carry
 
-    lax.fori_loop(0, chunks + 1, step_chunk, 0)
+    lax.fori_loop(0, chunks, step_chunk, 0)
 
     share_rows = shares.shape[1]
 
@@ -451,11 +448,7 @@
     sent_all(share_copy, sites)
     sent_all(total_copy, sites)
 
-    def sent_chunk(chunk, carry):
-        sent_all(functools.partial(piece_copy, chunk), count)
-        return carry
-
-    lax.fori_loop(0, chunks, sent_chunk, 0)
+    sent_all(functools.partial(piece_copy, chunks - 1), count)
 
 
 def per_device_fused(groups, sites, right_vectors, left_vectors, vacancy):

time: 147 us -> 164 us (1.12)
  Pallas kernels: 145 us -> 162 us
    pallas_call x1, Pallas kernels: 145 us -> 162 us  [per_device_fused(): call(right_vectors, left_vectors.reshape(2 * count_left * rows, width), v...]
where the time goes in v6:
time: 164 us
  Pallas kernels  162 us (99%)
  local copies, waits for them, and re-layouts  2.01 us (1%)
    pallas_call x1, Pallas kernels, per_device_fused(): call(right_vectors, left_vectors.reshape(2 * count_left * rows, width), v...  162 us

profile of v6, /device:TPU:0, one launch (start us, length us, event | category | flops | bytes accessed | tf_op | source)
XLA Modules:
  0.0 163.9 jit_solution(16149723922731309451)
XLA Ops:
  0.0 161.9 %shard_map.37 = f32[256,128]{1,0:T(8,128)} custom-call(f32[2,64,2,16,1,256]{5,4,3,2,1,0:T(1,128)} %right_ref.1, bf16[2048,512]{1,0:T(8,128)(2,1)} %bitcast.7, s32[16,512]{1,0:T(8,128)} %vacancy_ref.1), custom_call_target="tpu_custom_call" | custom-call | flops 2000000000 | bytes 8000000 | tf_op jit(solution)/shard_map/pallas_call | solution.py:493
  161.9 1.0 copy.5
  162.9 0.2 reshape.10
  163.1 0.8 copy.7
  (1 shorter events, 0.0 us)

commit v7 on v5

--- a/solution.py
+++ b/solution.py
@@ -132,7 +132,7 @@
 
 MESH = pl.DeviceIdType.MESH
 HALO = MOM
-COLS_AT_ONCE = 16
+COLS_AT_ONCE = 8
 LANES = 128
 
 
@@ -262,15 +262,17 @@
         turned = [pltpu.roll(v, 1, axis=1) for v in values]
         return [jnp.where(lane == 0, b, a) for a, b in zip(turned, [nothing] + turned[:-1])]
 
-    def sweep(source, target, earlier, mask, degree):
+    def sweep(chunk, source, target, earlier, mask, degree):
         first = degree + 1
+
+        base = pl.multiple_of(lax.rem(chunk, 2) * 2 * MOM * wide + degree * 2 * wide, 2 * wide)
 
         def one_row(row, odd_row):
             sign = -even_sign if odd_row else even_sign
             second, onsite = SECOND_HOP * sign, ONSITE_MASS * sign
             down = odd_lane != odd_row
             factor = [mask[row, :, at] for at in tiles]
-            halves = [[], []]
+            parts = []
             for part in range(0, wide, 8):
                 eight = slice(part, part + 8)
                 far, rest = [], []
@@ -310,13 +312,11 @@
                     if target is not None:
                         for v, at in zip(results, tiles):
                             target[row, r, eight, at] = v
-                    halves[r].append(results)
-            for r in (0, 1):
-                base = (r * MOM + degree) * wide
-                for i, at in enumerate(tiles):
-                    lanes = pl.ds(pl.multiple_of(row * width + at.start, LANES), LANES)
-                    block = jnp.concatenate([half[i] for half in halves[r]], axis=0)
-                    rounded[base : base + wide, lanes] = block.astype(jnp.bfloat16)
+                    parts.append(results)
+            for i, at in enumerate(tiles):
+                lanes = pl.ds(pl.multiple_of(row * width + at.start, LANES), LANES)
+                block = jnp.concatenate([part[i] for part in parts], axis=0)
+                rounded[pl.ds(base, 2 * wide), lanes] = block.astype(jnp.bfloat16)
 
         def pair(step, carry):
             one_row(first + 2 * step, first % 2 == 1)
@@ -365,10 +365,16 @@
             return carry
 
         lax.fori_loop(0, padded_rows, mask_row, 0)
-        sweep(field0, field1, None, present, 0)
-        sweep(field1, field2, None, scaled, 1)
-        sweep(field2, field3, field1, doubled, 2)
-        sweep(field3, None, field2, doubled, 3)
+        sweep(chunk, field0, field1, None, present, 0)
+        sweep(chunk, field1, field2, None, scaled, 1)
+        sweep(chunk, field2, field3, field1, doubled, 2)
+        sweep(chunk, field3, None, field2, doubled, 3)
+
+        @pl.when(lax.rem(chunk, 2) == 1)
+        def _():
+            multiply(chunk // 2)
+
+    def multiply(couple):
         product = lax.dot_general(
             left_flat[...],
             rounded[:, HALO * width : (HALO + rows) * width],
@@ -376,12 +382,12 @@
             preferred_element_type=jnp.float32,
         )
         count_left = product.shape[0] // 2
-        half = product.shape[1] // 2
         real, imaginary = product[:count_left], product[count_left:]
-        swapped = pltpu.roll(imaginary, half, axis=1)
-        wheres = lax.broadcasted_iota(jnp.int32, swapped.shape, 1)
-        combined = real + jnp.where(wheres < half, swapped, -swapped)
-        partial[pl.ds(pl.multiple_of(chunk * count_left, count_left), count_left), :] = combined
+        last = lax.rem(lax.broadcasted_iota(jnp.int32, imaginary.shape, 1), 2 * wide) >= wide
+        ahead = pltpu.roll(imaginary, imaginary.shape[1] - wide, axis=1)
+        behind = pltpu.roll(imaginary, wide, axis=1)
+        combined = real + jnp.where(last, -behind, ahead)
+        partial[pl.ds(pl.multiple_of(couple * count_left, count_left), count_left), :] = combined
 
     def step_chunk(step, carry):
         @pl.when(step < chunks)
@@ -466,7 +472,7 @@
     padded = rows + 2 * HALO
     field = pltpu.VMEM((padded, 2, wide, width), jnp.float32)
     mask = pltpu.VMEM((padded, 8, width), jnp.float32)
-    sums = (chunks * count_left, 2 * MOM * wide)
+    sums = (chunks // 2 * count_left, 4 * MOM * wide)
     dma = pltpu.SemaphoreType.DMA
     call = pl.pallas_call(
         functools.partial(fused_kernel, groups, sites),
@@ -480,7 +486,7 @@
         scratch_shapes=[
             pltpu.VMEM((chunks, padded, width // piece, 2, wide, piece), jnp.float32),
             field, field, field, field, mask, mask, mask,
-            pltpu.VMEM((2 * MOM * wide, padded * width), jnp.bfloat16),
+            pltpu.VMEM((4 * MOM * wide, padded * width), jnp.bfloat16),
             pltpu.VMEM((chunks, groups * sites, 2, wide, piece), jnp.float32),
             pltpu.VMEM((2 * count_left * rows, width), jnp.bfloat16),
             pltpu.VMEM((width // LANES, 2 * count_left * rows, LANES), jnp.float32),
@@ -498,17 +504,17 @@
         cost_estimate=pl.CostEstimate(flops=2 * 10**9, bytes_accessed=8 * 10**6, transcendentals=0),
     )
     summed = call(right_vectors, left_vectors.reshape(2 * count_left * rows, width), vacancy)
-    summed = summed.reshape(chunks, count_left, 2, MOM, wide)
-    return summed.transpose(2, 3, 1, 0, 4).reshape(2, MOM, count_left, width_group, 1)
+    summed = summed.reshape(chunks // 2, count_left, 2, MOM, 2, wide)
+    return summed.transpose(4, 3, 1, 0, 2, 5).reshape(2, MOM, count_left, width_group, 1)
 
 
 def per_device(groups, sites, right_vectors, left_vectors, vacancy):
     columns, piece = right_vectors.shape[1], right_vectors.shape[5]
     count_left, rows, width = left_vectors.shape[1:]
-    shares = (columns // COLS_AT_ONCE) * count_left
+    shares = columns // (2 * COLS_AT_ONCE) * count_left
     fits = (
         piece % 128 == 0 and width % piece == 0 and right_vectors.shape[4] == 1
-        and columns % COLS_AT_ONCE == 0 and rows % 2 == 0 and rows >= HALO
+        and columns % (2 * COLS_AT_ONCE) == 0 and rows % 2 == 0 and rows >= HALO
         and sites >= 4 and sites % 2 == 0 and shares % (8 * sites) == 0 and count_left % 8 == 0 and (2 * count_left * rows) % 16 == 0
     )
     if fits:

time: 147 us -> 147 us (level)
  no operation moved by 1% of the time
where the time goes in v7:
time: 147 us
  Pallas kernels  144 us (98%)
  local copies, waits for them, and re-layouts  2.01 us (1%)
    pallas_call x1, Pallas kernels, per_device_fused(): call(right_vectors, left_vectors.reshape(2 * count_left * rows, width), v...  144 us

profile of v7, /device:TPU:0, one launch (start us, length us, event | category | flops | bytes accessed | tf_op | source)
XLA Modules:
  0.0 146.5 jit_solution(17042956076014945302)
XLA Ops:
  0.0 144.5 %shard_map.37 = f32[256,128]{1,0:T(8,128)} custom-call(f32[2,64,2,16,1,256]{5,4,3,2,1,0:T(1,128)} %right_ref.1, bf16[2048,512]{1,0:T(8,128)(2,1)} %bitcast.7, s32[16,512]{1,0:T(8,128)} %vacancy_ref.1), custom_call_target="tpu_custom_call" | custom-call | flops 2000000000 | bytes 8000000 | tf_op jit(solution)/shard_map/pallas_call | solution.py:506
  144.5 1.0 copy.5
  145.5 0.2 reshape.10
  145.7 0.8 copy.7
  (1 shorter events, 0.0 us)

commit v8 on v7

--- a/solution.py
+++ b/solution.py
@@ -134,6 +134,7 @@
 HALO = MOM
 COLS_AT_ONCE = 8
 LANES = 128
+IN_FLIGHT = 3
 
 
 def fused_kernel(
@@ -236,7 +237,7 @@
 
     send_chunk(0, 0)
     lax.fori_loop(1, chunks, lay_out, 0)
-    lax.fori_loop(1, min(2, chunks), send_chunk, 0)
+    lax.fori_loop(1, min(IN_FLIGHT, chunks), send_chunk, 0)
 
     for copy in mask_copies():
         copy.wait()
@@ -347,9 +348,9 @@
         for copy in rim_copies(chunk):
             copy.start()
 
-        @pl.when(chunk + 2 < chunks)
+        @pl.when(chunk + IN_FLIGHT < chunks)
         def _():
-            send_chunk(chunk + 2, 0)
+            send_chunk(chunk + IN_FLIGHT, 0)
 
     def compute(chunk):
         for copy in rim_copies(chunk):

time: 147 us -> 153 us (1.041)
  Pallas kernels: 144 us -> 151 us
    pallas_call x1, Pallas kernels: 144 us -> 151 us  [per_device_fused(): call(right_vectors, left_vectors.reshape(2 * count_left * rows, width), v...]
where the time goes in v8:
time: 153 us
  Pallas kernels  151 us (99%)
  local copies, waits for them, and re-layouts  2.01 us (1%)
    pallas_call x1, Pallas kernels, per_device_fused(): call(right_vectors, left_vectors.reshape(2 * count_left * rows, width), v...  151 us

profile of v8, /device:TPU:0, one launch (start us, length us, event | category | flops | bytes accessed | tf_op | source)
XLA Modules:
  0.0 152.7 jit_solution(7883702540451617191)
XLA Ops:
  0.0 150.7 %shard_map.37 = f32[256,128]{1,0:T(8,128)} custom-call(f32[2,64,2,16,1,256]{5,4,3,2,1,0:T(1,128)} %right_ref.1, bf16[2048,512]{1,0:T(8,128)(2,1)} %bitcast.7, s32[16,512]{1,0:T(8,128)} %vacancy_ref.1), custom_call_target="tpu_custom_call" | custom-call | flops 2000000000 | bytes 8000000 | tf_op jit(solution)/shard_map/pallas_call | solution.py:507
  150.7 1.0 copy.5
  151.7 0.2 reshape.10
  151.9 0.8 copy.7
  (1 shorter events, 0.0 us)

commit v9 on v5

--- a/solution.py
+++ b/solution.py
@@ -236,7 +236,7 @@
 
     send_chunk(0, 0)
     lax.fori_loop(1, chunks, lay_out, 0)
-    lax.fori_loop(1, min(2, chunks), send_chunk, 0)
+    lax.fori_loop(1, min(2, chunks - 1), send_chunk, 0)
 
     for copy in mask_copies():
         copy.wait()
@@ -347,9 +347,13 @@
         for copy in rim_copies(chunk):
             copy.start()
 
-        @pl.when(chunk + 2 < chunks)
+        @pl.when(chunk + 2 < chunks - 1)
         def _():
             send_chunk(chunk + 2, 0)
+
+        @pl.when(chunk == chunks - 2)
+        def _():
+            send_chunk(chunks - 1, 0)
 
     def compute(chunk):
         for copy in rim_copies(chunk):
@@ -384,17 +388,17 @@
         partial[pl.ds(pl.multiple_of(chunk * count_left, count_left), count_left), :] = combined
 
     def step_chunk(step, carry):
-        @pl.when(step < chunks)
-        def _():
-            stage(step)
-
-        @pl.when(step > 0)
-        def _():
-            compute(step - 1)
-
-        return carry
-
-    lax.fori_loop(0, chunks + 1, step_chunk, 0)
+        stage(step)
+
+        def work(chunk, inner):
+            compute(chunk)
+            return inner
+
+        start = jnp.where(step < chunks - 1, jnp.maximum(step - 1, 0), step)
+        lax.fori_loop(start, jnp.where(step < chunks - 2, step, step + 1), work, 0)
+        return carry
+
+    lax.fori_loop(0, chunks, step_chunk, 0)
 
     share_rows = shares.shape[1]
 
@@ -509,7 +513,7 @@
     fits = (
         piece % 128 == 0 and width % piece == 0 and right_vectors.shape[4] == 1
         and columns % COLS_AT_ONCE == 0 and rows % 2 == 0 and rows >= HALO
-        and sites >= 4 and sites % 2 == 0 and shares % (8 * sites) == 0 and count_left % 8 == 0 and (2 * count_left * rows) % 16 == 0
+        and sites >= 4 and columns >= 2 * COLS_AT_ONCE and sites % 2 == 0 and shares % (8 * sites) == 0 and count_left % 8 == 0 and (2 * count_left * rows) % 16 == 0
     )
     if fits:
         return per_device_fused(groups, sites, right_vectors, left_vectors, vacancy)

time: 147 us -> 142 us (0.966)
  Pallas kernels: 145 us -> 140 us
    pallas_call x1, Pallas kernels: 145 us -> 140 us  [per_device_fused(): call(right_vectors, left_vectors.reshape(2 * count_left * rows, width), v...]
where the time goes in v9:
time: 142 us
  Pallas kernels  140 us (99%)
  local copies, waits for them, and re-layouts  2.01 us (1%)
    pallas_call x1, Pallas kernels, per_device_fused(): call(right_vectors, left_vectors.reshape(2 * count_left * rows, width), v...  140 us

profile of v9, /device:TPU:0, one launch (start us, length us, event | category | flops | bytes accessed | tf_op | source)
XLA Modules:
  0.0 141.8 jit_solution(3770338009382855736)
XLA Ops:
  0.0 139.8 %shard_map.37 = f32[256,128]{1,0:T(8,128)} custom-call(f32[2,64,2,16,1,256]{5,4,3,2,1,0:T(1,128)} %right_ref.1, bf16[2048,512]{1,0:T(8,128)(2,1)} %bitcast.7, s32[16,512]{1,0:T(8,128)} %vacancy_ref.1), custom_call_target="tpu_custom_call" | custom-call | flops 2000000000 | bytes 8000000 | tf_op jit(solution)/shard_map/pallas_call | solution.py:504
  139.8 1.0 copy.5
  140.8 0.2 reshape.10
  141.0 0.8 copy.7
  (1 shorter events, 0.0 us)
